TPU v7x, 512 devices: a whole 4x8x8 slice. The times are simulated.
512 devices in a mesh: dp: 64 (over z, x, core), mp: 8 (over y).
Axes of the slice: x: 4, y: 8, z: 8, core: 2. Of those that a mesh axis runs over, the one named last changes fastest.
Arguments:
- activations: bfloat16 [8, 128, 64, 5120], P('mp', 'dp'), may hold values from -6 to 6
- out_grads: bfloat16 [8, 128, 64, 5120], P('mp', 'dp'), may hold values from -6 to 6
- proj_in: bfloat16 [8, 64, 5120], P('mp'), may hold values from -0.078125 to 0.078125
- proj_out: bfloat16 [8, 64, 5120], P('mp'), may hold values from -0.078125 to 0.078125
- query_feat: float32 [8, 1024, 4096], P('mp', 'dp'), may hold values from -6 to 6
- candidates: int32 [64, 8], P('dp'), may hold values from 0 to 63
Outputs:
- gram: float32 [8, 4096, 4096], P('mp', 'dp')
- influence: float32 [1024, 16], P('dp')
Inputs may be any that keep to these rules, and one draw needn't show every extreme that they name: `candidates`: each entry names a training shard; duplicates may occur.
All inputs are finite; a program needn't handle non-finite values.
Results may differ from a plain program's by a relative error of at most 0.0089.
Values may be sent and summed in bfloat16 or wider, within the bound.
A program may use at most 64 MiB of HBM per device.

v0:
```python
import functools

import jax
import jax.numpy as jnp
from jax import lax
from jax.experimental import pallas as pl
from jax.experimental.pallas import tpu as pltpu
from jax.sharding import PartitionSpec as P

ITERS = 6
NZ, NX, NC = 8, 4, 2
GROUPS = NX * NC
CHUNKS = 4
MESH = pl.DeviceIdType.MESH
F32 = jnp.float32
BF16 = jnp.bfloat16
Z_ORDER = (1, 7, 2, 6, 3, 5, 4)


def dot_nt(lhs, rhs):
    return lax.dot_general(lhs, rhs, (((1,), (1,)), ((), ())), preferred_element_type=F32)


def dot_nn(lhs, rhs):
    return jnp.dot(lhs, rhs, preferred_element_type=F32)


def high_low(value):
    high = value.astype(BF16)
    return high, (value - high.astype(F32)).astype(BF16)


def kernel(
    cand_ref, act_hbm, grad_hbm, pin_hbm, pout_hbm, query_hbm,
    gram_hbm, infl_ref,
    act, grad, pin, pout, query, raw, wide, feats, turned, lhs_query, gram, parts,
    in_sem, query_sem, send_sem, z_sem, raw_sem, part_send, part_sem, gram_sem,
):
    dp = lax.axis_index("dp")
    mp = lax.axis_index("mp")
    modules = parts.shape[0]
    zi, group = dp // GROUPS, dp % GROUPS
    xi, core = group // NC, group % NC

    width = act.shape[1] // CHUNKS
    loads = []
    for chunk in range(CHUNKS):
        cols = pl.ds(chunk * width, width)
        row = []
        for which, (src, dst) in enumerate(((pout_hbm, pout), (grad_hbm, grad), (pin_hbm, pin), (act_hbm, act))):
            row.append(pltpu.make_async_copy(src.at[:, cols], dst.at[:, cols], in_sem.at[chunk, which]))
        loads.append(row)
        for copy in row:
            copy.start()
    query_load = pltpu.make_async_copy(query_hbm, query, query_sem)
    query_load.start()

    def dp_at(z, g):
        return {"dp": z * GROUPS + g}

    mate = dp_at(zi, xi * NC + (1 - core))
    z_peer = [(zi + step) % NZ for step in range(NZ)]
    x_peer = [((xi + step) % NX) * NC + core for step in range(NX)]
    m_peer = [(mp + step) % modules for step in range(modules)]

    barrier = pltpu.get_barrier_semaphore()
    for step in range(1, NZ):
        pl.semaphore_signal(barrier, 1, device_id=dp_at(z_peer[step], group), device_id_type=MESH)
    for step in range(1, NX):
        pl.semaphore_signal(barrier, 1, device_id=dp_at(zi, x_peer[step]), device_id_type=MESH)
    pl.semaphore_signal(barrier, 1, device_id=mate, device_id_type=MESH)
    for step in range(1, modules):
        pl.semaphore_signal(barrier, 1, device_id={"mp": m_peer[step]}, device_id_type=MESH)

    gout = jnp.zeros((pout.shape[0], grad.shape[0]), F32)
    xin = jnp.zeros((act.shape[0], 2 * pin.shape[0]), F32)
    for chunk in range(CHUNKS):
        cols = slice(chunk * width, (chunk + 1) * width)
        loads[chunk][0].wait()
        loads[chunk][1].wait()
        gout += dot_nt(pout[:, cols], grad[:, cols])
        loads[chunk][2].wait()
        loads[chunk][3].wait()
        pin_cols = pin[:, cols]
        xin += dot_nt(act[:, cols], jnp.concatenate([pin_cols, pin_cols], axis=0))

    rank = pout.shape[0]
    half = rank // 2
    turned[...] = gout
    stacked = jnp.concatenate(
        [turned[pl.ds(0, half, stride=2), :], turned[pl.ds(1, half, stride=2), :]], axis=0
    ).astype(BF16)
    token = lax.broadcasted_iota(jnp.int32, xin.shape, 0)
    tokens = act.shape[0] // 2
    both = jnp.concatenate(
        [jnp.where(token < tokens, xin, 0.0), jnp.where(token >= tokens, xin, 0.0)], axis=1
    ).astype(BF16)
    joined = dot_nn(stacked, both)
    lane = lax.broadcasted_iota(jnp.int32, (half, 2 * rank), 1)
    own = [
        jnp.where(lane < rank, joined[:half, s * 2 * rank:(s + 1) * 2 * rank], joined[half:, s * 2 * rank:(s + 1) * 2 * rank])
        for s in range(2)
    ]
    raw[group * NZ + zi] = jnp.concatenate(own, axis=0).astype(BF16)

    pl.semaphore_wait(barrier, (NZ - 1) + (NX - 1) + 1 + (modules - 1))

    def move(g, z, target, arrival):
        return pltpu.make_async_remote_copy(
            src_ref=raw.at[g * NZ + z], dst_ref=raw.at[g * NZ + z], send_sem=send_sem, recv_sem=arrival,
            device_id=target, device_id_type=MESH,
        )

    def spread(z):
        for step in range(1, NX):
            move(group, z, dp_at(zi, x_peer[step]), raw_sem.at[group, z]).start()
        move(group, z, mate, raw_sem.at[group, z]).start()

    def relay(z):
        for step in range(1, NX):
            g = x_peer[step]
            move(g, z, mate, raw_sem.at[g, z]).wait_recv()
            move(g, z, mate, raw_sem.at[g, z]).start()

    for step in Z_ORDER:
        move(group, zi, dp_at(z_peer[step], group), z_sem.at[zi]).start()
    spread(zi)
    query_load.wait()
    query_high, query_low = high_low(query[...])
    lhs_query[:16, :] = query_high
    lhs_query[16:, :] = query_low
    query_sq = jnp.sum(query[...] * query[...], axis=1, keepdims=True)

    before = zi
    for step in Z_ORDER:
        z = (zi - step + NZ) % NZ
        move(group, z, mate, z_sem.at[z]).wait_recv()
        spread(z)
        relay(before)
        before = z
    relay(before)
    for step in range(NX):
        g = ((xi + step) % NX) * NC + (1 - core)
        for z in range(NZ):
            move(g, z, mate, raw_sem.at[g, z]).wait_recv()

    rows = half
    seqs = GROUPS * NZ * 2
    wide[...] = raw[...].reshape(seqs * rows, 2 * rank).astype(F32)
    for r in range(rows):
        feats[:, r * 128:(r + 1) * 128] = wide[pl.ds(r, seqs, stride=rows), :].astype(BF16)
    tile = feats[...]
    inner = dot_nt(jnp.concatenate([tile, lhs_query[...]], axis=0), tile)
    kmat = inner[:seqs]
    u = inner[seqs:seqs + 16] + inner[seqs + 16:]
    eye = lax.broadcasted_iota(jnp.int32, (seqs, seqs), 0) == lax.broadcasted_iota(jnp.int32, (seqs, seqs), 1)
    trace = jnp.sum(jnp.sum(jnp.where(eye, kmat, 0.0), axis=1, keepdims=True), axis=0, keepdims=True)
    damping = 0.1 * trace / (rows * 2 * rank)
    k_high, k_low = high_low(kmat)
    k_both = jnp.concatenate([k_high, k_low], axis=1)

    def apply_k(v):
        v_high, v_low = high_low(v)
        out = dot_nn(jnp.concatenate([v_high, v_low], axis=0), k_both)
        return out[:16, :seqs] + (out[:16, seqs:] + out[16:, :seqs])

    w, v = u, u
    y = jnp.zeros_like(u)
    y_dir = jnp.zeros_like(u)
    c = jnp.ones_like(query_sq)
    c_dir = jnp.ones_like(query_sq)
    resid_sq, dir_sq = query_sq, query_sq
    scores = jnp.zeros_like(u)
    selfterm = jnp.zeros_like(query_sq)
    for iteration in range(ITERS):
        alpha = resid_sq / (jnp.sum(v * v, axis=1, keepdims=True) + damping * dir_sq)
        scores = scores + alpha * v
        selfterm = selfterm + alpha * resid_sq
        if iteration == ITERS - 1:
            break
        image = apply_k(v) + damping * v
        w = w - alpha * image
        y = y - alpha * (v + damping * y_dir)
        c = c - alpha * damping * c_dir
        next_sq = c * c * query_sq + jnp.sum(y * (c * u + w), axis=1, keepdims=True)
        beta = next_sq / resid_sq
        v = w + beta * v
        y_dir = y + beta * y_dir
        c_dir = c + beta * c_dir
        dir_sq = next_sq + beta * beta * dir_sq
        resid_sq = next_sq

    col = lax.broadcasted_iota(jnp.int32, (seqs, 128), 1)
    spot = jnp.full((seqs, 128), -1, jnp.int32)
    cands = cand_ref.shape[1]
    for i in range(cands):
        shard = cand_ref[0, i]
        first = (shard % GROUPS) * (2 * NZ) + (shard // GROUPS) * 2
        spot = jnp.where(col // 2 == i, first + col % 2, spot)
    pick = jnp.where(lax.broadcasted_iota(jnp.int32, (seqs, 128), 0) == spot, 1.0, 0.0).astype(BF16)
    s_high, s_low = high_low(scores)
    s_last = (scores - s_high.astype(F32) - s_low.astype(F32)).astype(BF16)
    picked = dot_nn(jnp.concatenate([s_high, s_low, s_last], axis=0), pick)
    picked = picked[:16] + picked[16:32] + picked[32:]
    part_col = lax.broadcasted_iota(jnp.int32, (16, 128), 1)
    parts[mp] = jnp.where(part_col == 2 * cands, selfterm, picked)
    for step in range(1, modules):
        pltpu.make_async_remote_copy(
            src_ref=parts.at[mp], dst_ref=parts.at[mp], send_sem=part_send, recv_sem=part_sem.at[mp],
            device_id={"mp": m_peer[step]}, device_id_type=MESH,
        ).start()

    own_tile = feats[:, pl.ds(pl.multiple_of((dp // 2) * 128, 128), 128)].astype(F32).T
    own_rows = jnp.where(dp % 2 == 0, own_tile[:rank], own_tile[rank:]).astype(BF16)
    gram_chunks = 4
    gram_width = gram.shape[1] // gram_chunks
    stores = []
    for chunk in range(gram_chunks):
        cols = slice(chunk * gram_width, (chunk + 1) * gram_width)
        gram[:, cols] = dot_nn(own_rows, feats[:, cols])
        at = pl.ds(chunk * gram_width, gram_width)
        stores.append(pltpu.make_async_copy(gram.at[:, at], gram_hbm.at[:, at], gram_sem.at[chunk]))
        stores[-1].start()

    for step in range(1, modules):
        other = m_peer[step]
        pltpu.make_async_remote_copy(
            src_ref=parts.at[other], dst_ref=parts.at[other], send_sem=part_send, recv_sem=part_sem.at[other],
            device_id={"mp": other}, device_id_type=MESH,
        ).wait_recv()
    total = parts[0]
    for m in range(1, modules):
        total = total + parts[m]
    infl_ref[...] = total[:, :2 * cands] / jnp.sqrt(total[:, 2 * cands:2 * cands + 1])

    def all_sent(ref, count, sem):
        pltpu.make_async_remote_copy(
            src_ref=ref.at[pl.ds(0, count)], dst_ref=ref.at[pl.ds(0, count)], send_sem=sem, recv_sem=z_sem.at[0],
            device_id=mate, device_id_type=MESH,
        ).wait_send()

    all_sent(raw, NX * NZ + NZ * (NX - 1) + NZ - 1, send_sem)
    all_sent(parts, modules - 1, part_send)
    for copy in stores:
        copy.wait()


def on_device(activations, out_grads, proj_in, proj_out, query_feat, candidates):
    _, seqs, tokens, depth = activations.shape
    rank = proj_in.shape[1]
    queries, size = query_feat.shape[1:]
    modules = lax.axis_size("mp")
    shards = lax.axis_size("dp")
    total = shards * seqs
    vmem = pltpu.VMEM
    dma = pltpu.SemaphoreType.DMA
    gram, influence = pl.pallas_call(
        kernel,
        name="influence",
        out_shape=(
            jax.ShapeDtypeStruct((size // shards, size), F32),
            jax.ShapeDtypeStruct((queries, candidates.shape[1] * seqs), F32),
        ),
        in_specs=[pl.BlockSpec(memory_space=pltpu.SMEM)] + [pl.BlockSpec(memory_space=pl.ANY)] * 5,
        out_specs=(pl.BlockSpec(memory_space=pl.ANY), pl.BlockSpec(memory_space=pltpu.VMEM)),
        scratch_shapes=[
            vmem((seqs * tokens, depth), BF16),
            vmem((seqs * tokens, depth), BF16),
            vmem((rank, depth), BF16),
            vmem((rank, depth), BF16),
            vmem((queries, size), F32),
            vmem((GROUPS * NZ, seqs * size // 128, 128), BF16),
            vmem((total * size // 128, 128), F32),
            vmem((total, size), BF16),
            vmem((rank, seqs * tokens), F32),
            vmem((2 * queries, size), BF16),
            vmem((size // shards, size), F32),
            vmem((modules, queries, 128), F32),
            dma((CHUNKS, 4)),
            dma,
            dma,
            dma((NZ,)),
            dma((GROUPS, NZ)),
            dma,
            dma((modules,)),
            dma((4,)),
        ],
        compiler_params=pltpu.CompilerParams(
            collective_id=0, has_side_effects=True, vmem_limit_bytes=48 * 2**20
        ),
    )(
        candidates,
        activations.reshape(seqs * tokens, depth),
        out_grads.reshape(seqs * tokens, depth),
        proj_in.reshape(rank, depth),
        proj_out.reshape(rank, depth),
        query_feat.reshape(queries, size),
    )
    return gram[None], influence


def solution(mesh):
    placed = (
        P("mp", "dp", None, None),
        P("mp", "dp", None, None),
        P("mp", None, None),
        P("mp", None, None),
        P("mp", "dp", None),
        P("dp", None),
    )
    return jax.shard_map(
        on_device,
        mesh=mesh,
        in_specs=placed,
        out_specs=(P("mp", "dp", None), P("dp", None)),
        check_vma=False,
    )
```

profile of v0, /device:TPU:1, one launch (start us, length us, event | category | flops | bytes accessed | tf_op | source)
XLA Modules:
  0.0 52.8 jit_solution(9432949005861929455)
XLA Ops:
  0.6 0.0 copy-start
  0.6 1.3 %copy-done = bf16[1,2,64,5120]{3,2,1,0:T(8,128)(2,1)S(1)} copy-done((bf16[1,2,64,5120]{3,2,1,0:T(8,128)(2,1)S(1)}, bf16[1,2,64,5120]{3,2,1,0:T(8,128)(2,1)}, u32[]{:S(2)}) %copy-start) | copy-done | bytes 1310744
  1.9 0.0 copy-start.1
  2.0 1.3 %copy-done.1 = bf16[1,2,64,5120]{3,2,1,0:T(8,128)(2,1)S(1)} copy-done((bf16[1,2,64,5120]{3,2,1,0:T(8,128)(2,1)S(1)}, bf16[1,2,64,5120]{3,2,1,0:T(8,128)(2,1)}, u32[]{:S(2)}) %copy-start.1) | copy-done | bytes 1310744
  3.3 0.0 copy-start.2
  3.3 1.1 %copy-done.2 = bf16[1,64,5120]{2,1,0:T(8,128)(2,1)S(1)} copy-done((bf16[1,64,5120]{2,1,0:T(8,128)(2,1)S(1)}, bf16[1,64,5120]{2,1,0:T(8,128)(2,1)}, u32[]{:S(2)}) %copy-start.2) | copy-done | bytes 655384
  4.4 0.0 copy-start.3
  4.4 1.1 %copy-done.3 = bf16[1,64,5120]{2,1,0:T(8,128)(2,1)S(1)} copy-done((bf16[1,64,5120]{2,1,0:T(8,128)(2,1)S(1)}, bf16[1,64,5120]{2,1,0:T(8,128)(2,1)}, u32[]{:S(2)}) %copy-start.3) | copy-done | bytes 655384
  5.4 0.0 copy-start.4
  5.4 0.9 %copy-done.4 = f32[1,16,4096]{2,1,0:T(8,128)S(1)} copy-done((f32[1,16,4096]{2,1,0:T(8,128)S(1)}, f32[1,16,4096]{2,1,0:T(8,128)}, u32[]{:S(2)}) %copy-start.4) | copy-done | bytes 262168
  6.4 0.0 copy-start.5
  6.4 0.7 %copy-done.5 = s32[1,8]{1,0:T(1,128)S(1)} copy-done((s32[1,8]{1,0:T(1,128)S(1)}, s32[1,8]{1,0:T(1,128)}, u32[]{:S(2)}) %copy-start.5) | copy-done | bytes 56
  7.0 44.2 %influence.1 = (f32[64,4096]{1,0:T(8,128)S(1)}, f32[16,16]{1,0:T(8,128)S(1)}) custom-call(s32[1,8]{1,0:T(1,128)S(1)} %copy-done.5, bf16[128,5120]{1,0:T(8,128)(2,1)S(1)} %bitcast.6, bf16[128,5120]{1,0:T(8,128)(2,1)S(1)} %bitcast.7, bf16[64,5120]{1,0:T(8,128)(2,1)S(1)} %bitcast.9, bf16[64,5120]{1,0:T(8,128)(2,1)S(1)} %bitcast.10, f32[16,4096]{1,0:T(8,128)S(1)} %bitcast.11), custom_call_target="tpu_custom_call" | custom-call | tf_op jit(solution)/shard_map/influence/pallas_call | solution.py:257
  51.2 1.0 %copy.10 = f32[1,64,4096]{2,1,0:T(8,128)} copy(f32[1,64,4096]{2,1,0:T(8,128)S(1)} %bitcast.8) | data formatting | bytes 2097152
  52.2 0.6 %copy.11 = f32[16,16]{1,0:T(8,128)} copy(f32[16,16]{1,0:T(8,128)S(1)} %get-tuple-element.9) | data formatting | bytes 2048
Async XLA Ops:
  0.6 1.3 %copy-start = (bf16[1,2,64,5120]{3,2,1,0:T(8,128)(2,1)S(1)}, bf16[1,2,64,5120]{3,2,1,0:T(8,128)(2,1)}, u32[]{:S(2)}) copy-start(bf16[1,2,64,5120]{3,2,1,0:T(8,128)(2,1)} %param.6) | copy-start | bytes 3932164
  1.9 1.3 %copy-start.1 = (bf16[1,2,64,5120]{3,2,1,0:T(8,128)(2,1)S(1)}, bf16[1,2,64,5120]{3,2,1,0:T(8,128)(2,1)}, u32[]{:S(2)}) copy-start(bf16[1,2,64,5120]{3,2,1,0:T(8,128)(2,1)} %param.7) | copy-start | bytes 3932164
  3.3 1.1 %copy-start.2 = (bf16[1,64,5120]{2,1,0:T(8,128)(2,1)S(1)}, bf16[1,64,5120]{2,1,0:T(8,128)(2,1)}, u32[]{:S(2)}) copy-start(bf16[1,64,5120]{2,1,0:T(8,128)(2,1)} %param.8) | copy-start | bytes 1966084
  4.4 1.1 %copy-start.3 = (bf16[1,64,5120]{2,1,0:T(8,128)(2,1)S(1)}, bf16[1,64,5120]{2,1,0:T(8,128)(2,1)}, u32[]{:S(2)}) copy-start(bf16[1,64,5120]{2,1,0:T(8,128)(2,1)} %param.9) | copy-start | bytes 1966084
  5.4 0.9 %copy-start.4 = (f32[1,16,4096]{2,1,0:T(8,128)S(1)}, f32[1,16,4096]{2,1,0:T(8,128)}, u32[]{:S(2)}) copy-start(f32[1,16,4096]{2,1,0:T(8,128)} %param.10) | copy-start | bytes 786436
  6.4 0.7 %copy-start.5 = (s32[1,8]{1,0:T(1,128)S(1)}, s32[1,8]{1,0:T(1,128)}, u32[]{:S(2)}) copy-start(s32[1,8]{1,0:T(1,128)} %cand_ref.1) | copy-start | bytes 100
where the time goes:
time: 53.1 us; the launch traced here: 52.8 us
  Pallas kernels  44.2 us (83%)
  local copies, waits for them, and re-layouts  7.97 us (15%)
  between operations  0.65 us (1%)
    pallas_call x1, Pallas kernels, on_device(): pl.pallas_call(kernel, name='influence', out_shape=(jax.ShapeDtypeStruct(...  44.2 us
    unnamed x14, local copies, waits for them, and re-layouts  7.97 us

commit v1 on v0

--- a/solution.py
+++ b/solution.py
@@ -14,7 +14,10 @@
 MESH = pl.DeviceIdType.MESH
 F32 = jnp.float32
 BF16 = jnp.bfloat16
-Z_ORDER = (1, 7, 2, 6, 3, 5, 4)
+X_ORDER = (1, 3, 2)
+SLOTS = (0, 1, 7, 2, 6, 3, 5, 4)
+DIRECT = (1, 7)
+WAVES = ((2, 6), (3, 5, 4))
 
 
 def dot_nt(lhs, rhs):
@@ -31,10 +34,10 @@
 
 
 def kernel(
-    cand_ref, act_hbm, grad_hbm, pin_hbm, pout_hbm, query_hbm,
-    gram_hbm, infl_ref,
-    act, grad, pin, pout, query, raw, wide, feats, turned, lhs_query, gram, parts,
-    in_sem, query_sem, send_sem, z_sem, raw_sem, part_send, part_sem, gram_sem,
+    cand_hbm, act_hbm, grad_hbm, pin_hbm, pout_hbm, query_hbm,
+    gram_ref, infl_ref,
+    cand, act, grad, pin, pout, query, raw, wide, feats, turned, lhs_query, parts,
+    in_sem, query_sem, cand_sem, send_sem, block_sem, wave_sem, relay_sem, part_send, part_sem,
 ):
     dp = lax.axis_index("dp")
     mp = lax.axis_index("mp")
@@ -54,6 +57,8 @@
             copy.start()
     query_load = pltpu.make_async_copy(query_hbm, query, query_sem)
     query_load.start()
+    cand_load = pltpu.make_async_copy(cand_hbm, cand, cand_sem)
+    cand_load.start()
 
     def dp_at(z, g):
         return {"dp": z * GROUPS + g}
@@ -68,6 +73,9 @@
         pl.semaphore_signal(barrier, 1, device_id=dp_at(z_peer[step], group), device_id_type=MESH)
     for step in range(1, NX):
         pl.semaphore_signal(barrier, 1, device_id=dp_at(zi, x_peer[step]), device_id_type=MESH)
+    for distance in DIRECT:
+        for step in range(1, NX):
+            pl.semaphore_signal(barrier, 1, device_id=dp_at(z_peer[distance], x_peer[step]), device_id_type=MESH)
     pl.semaphore_signal(barrier, 1, device_id=mate, device_id_type=MESH)
     for step in range(1, modules):
         pl.semaphore_signal(barrier, 1, device_id={"mp": m_peer[step]}, device_id_type=MESH)
@@ -101,54 +109,83 @@
         jnp.where(lane < rank, joined[:half, s * 2 * rank:(s + 1) * 2 * rank], joined[half:, s * 2 * rank:(s + 1) * 2 * rank])
         for s in range(2)
     ]
-    raw[group * NZ + zi] = jnp.concatenate(own, axis=0).astype(BF16)
-
-    pl.semaphore_wait(barrier, (NZ - 1) + (NX - 1) + 1 + (modules - 1))
-
-    def move(g, z, target, arrival):
+    raw[group * NZ] = jnp.concatenate(own, axis=0).astype(BF16)
+
+    pl.semaphore_wait(barrier, (NZ - 1) + (1 + len(DIRECT)) * (NX - 1) + 1 + (modules - 1))
+
+    def remote(src, dst, target, arrival):
         return pltpu.make_async_remote_copy(
-            src_ref=raw.at[g * NZ + z], dst_ref=raw.at[g * NZ + z], send_sem=send_sem, recv_sem=arrival,
-            device_id=target, device_id_type=MESH,
+            src_ref=src, dst_ref=dst, send_sem=send_sem, recv_sem=arrival, device_id=target, device_id_type=MESH
         )
 
-    def spread(z):
-        for step in range(1, NX):
-            move(group, z, dp_at(zi, x_peer[step]), raw_sem.at[group, z]).start()
-        move(group, z, mate, raw_sem.at[group, z]).start()
-
-    def relay(z):
-        for step in range(1, NX):
-            g = x_peer[step]
-            move(g, z, mate, raw_sem.at[g, z]).wait_recv()
-            move(g, z, mate, raw_sem.at[g, z]).start()
-
-    for step in Z_ORDER:
-        move(group, zi, dp_at(z_peer[step], group), z_sem.at[zi]).start()
-    spread(zi)
+    def blocks(g, first, count):
+        return raw.at[pl.ds(g * NZ + first, count)]
+
+    def send_own(distance, step):
+        slot = SLOTS.index(distance)
+        target = dp_at(z_peer[(NZ - distance) % NZ], x_peer[step])
+        remote(blocks(group, 0, 1), blocks(group, slot, 1), target, block_sem.at[group, slot]).start()
+
+    def wait_block(g, slot):
+        remote(blocks(g, slot, 1), blocks(g, slot, 1), mate, block_sem.at[g, slot]).wait_recv()
+
+    def wave(g, number, target):
+        slots = [SLOTS.index(distance) for distance in WAVES[number]]
+        at = blocks(g, slots[0], len(slots))
+        return remote(at, at, target, wave_sem.at[g, number])
+
+    def relay(g):
+        return remote(blocks(g, 0, NZ), blocks(g, 0, NZ), mate, relay_sem.at[g])
+
+    for step in X_ORDER:
+        send_own(0, step)
+    for distance in (4, 3, 5, 2, 6, 1, 7):
+        send_own(distance, 0)
+    for distance in DIRECT:
+        for step in X_ORDER:
+            send_own(distance, step)
     query_load.wait()
+    cand_load.wait()
     query_high, query_low = high_low(query[...])
     lhs_query[:16, :] = query_high
     lhs_query[16:, :] = query_low
     query_sq = jnp.sum(query[...] * query[...], axis=1, keepdims=True)
 
-    before = zi
-    for step in Z_ORDER:
-        z = (zi - step + NZ) % NZ
-        move(group, z, mate, z_sem.at[z]).wait_recv()
-        spread(z)
-        relay(before)
-        before = z
-    relay(before)
-    for step in range(NX):
-        g = ((xi + step) % NX) * NC + (1 - core)
-        for z in range(NZ):
-            move(g, z, mate, raw_sem.at[g, z]).wait_recv()
-
     rows = half
     seqs = GROUPS * NZ * 2
-    wide[...] = raw[...].reshape(seqs * rows, 2 * rank).astype(F32)
-    for r in range(rows):
-        feats[:, r * 128:(r + 1) * 128] = wide[pl.ds(r, seqs, stride=rows), :].astype(BF16)
+    group_rows = NZ * 2 * rows
+    group_seqs = NZ * 2
+
+    def lay_out(place, g):
+        base = place * group_rows
+        wide[base:base + group_rows] = raw[pl.ds(g * NZ, NZ)].reshape(group_rows, 2 * rank).astype(F32)
+        at = pl.ds(pl.multiple_of(g * group_seqs, group_seqs), group_seqs)
+        for r in range(rows):
+            feats[at, r * 128:(r + 1) * 128] = wide[pl.ds(base + r, group_seqs, stride=rows), :].astype(BF16)
+
+    for number in range(len(WAVES)):
+        for distance in WAVES[number]:
+            wait_block(group, SLOTS.index(distance))
+        for step in X_ORDER:
+            wave(group, number, dp_at(zi, x_peer[step])).start()
+    for distance in DIRECT:
+        wait_block(group, SLOTS.index(distance))
+    relay(group).start()
+    lay_out(0, group)
+    for place, step in enumerate(X_ORDER):
+        g = x_peer[step]
+        wait_block(g, 0)
+        for distance in DIRECT:
+            wait_block(g, SLOTS.index(distance))
+        for number in range(len(WAVES)):
+            wave(g, number, mate).wait_recv()
+        relay(g).start()
+        lay_out(1 + place, g)
+    for place, step in enumerate((0,) + X_ORDER):
+        g = ((xi + step) % NX) * NC + (1 - core)
+        relay(g).wait_recv()
+        lay_out(NX + place, g)
+
     tile = feats[...]
     inner = dot_nt(jnp.concatenate([tile, lhs_query[...]], axis=0), tile)
     kmat = inner[:seqs]
@@ -192,10 +229,12 @@
 
     col = lax.broadcasted_iota(jnp.int32, (seqs, 128), 1)
     spot = jnp.full((seqs, 128), -1, jnp.int32)
-    cands = cand_ref.shape[1]
+    cands = cand.shape[1]
     for i in range(cands):
-        shard = cand_ref[0, i]
-        first = (shard % GROUPS) * (2 * NZ) + (shard // GROUPS) * 2
+        shard = cand[0, i]
+        distance = (shard // GROUPS + NZ - zi) % NZ
+        slot = jnp.where(distance == 0, 0, jnp.where(distance <= NZ // 2, 2 * distance - 1, 2 * (NZ - distance)))
+        first = (shard % GROUPS) * group_seqs + slot * 2
         spot = jnp.where(col // 2 == i, first + col % 2, spot)
     pick = jnp.where(lax.broadcasted_iota(jnp.int32, (seqs, 128), 0) == spot, 1.0, 0.0).astype(BF16)
     s_high, s_low = high_low(scores)
@@ -213,14 +252,10 @@
     own_tile = feats[:, pl.ds(pl.multiple_of((dp // 2) * 128, 128), 128)].astype(F32).T
     own_rows = jnp.where(dp % 2 == 0, own_tile[:rank], own_tile[rank:]).astype(BF16)
     gram_chunks = 4
-    gram_width = gram.shape[1] // gram_chunks
-    stores = []
+    gram_width = gram_ref.shape[1] // gram_chunks
     for chunk in range(gram_chunks):
         cols = slice(chunk * gram_width, (chunk + 1) * gram_width)
-        gram[:, cols] = dot_nn(own_rows, feats[:, cols])
-        at = pl.ds(chunk * gram_width, gram_width)
-        stores.append(pltpu.make_async_copy(gram.at[:, at], gram_hbm.at[:, at], gram_sem.at[chunk]))
-        stores[-1].start()
+        gram_ref[:, cols] = dot_nn(own_rows, feats[:, cols])
 
     for step in range(1, modules):
         other = m_peer[step]
@@ -235,14 +270,23 @@
 
     def all_sent(ref, count, sem):
         pltpu.make_async_remote_copy(
-            src_ref=ref.at[pl.ds(0, count)], dst_ref=ref.at[pl.ds(0, count)], send_sem=sem, recv_sem=z_sem.at[0],
+            src_ref=ref.at[pl.ds(0, count)], dst_ref=ref.at[pl.ds(0, count)], send_sem=sem, recv_sem=relay_sem.at[0],
             device_id=mate, device_id_type=MESH,
         ).wait_send()
 
-    all_sent(raw, NX * NZ + NZ * (NX - 1) + NZ - 1, send_sem)
+    own_copies = (NX - 1) + (NZ - 1) + len(DIRECT) * (NX - 1)
+    wave_copies = sum(len(distances) for distances in WAVES) * (NX - 1)
+    all_sent(raw, own_copies + wave_copies + NX * NZ, send_sem)
     all_sent(parts, modules - 1, part_send)
-    for copy in stores:
-        copy.wait()
+
+
+def write_kernel(gram_ref, infl_ref, gram_out, infl_out, gram_sem, infl_sem):
+    gram_copy = pltpu.make_async_copy(gram_ref, gram_out, gram_sem)
+    infl_copy = pltpu.make_async_copy(infl_ref, infl_out, infl_sem)
+    gram_copy.start()
+    infl_copy.start()
+    infl_copy.wait()
+    gram_copy.wait()
 
 
 def on_device(activations, out_grads, proj_in, proj_out, query_feat, candidates):
@@ -261,9 +305,10 @@
             jax.ShapeDtypeStruct((size // shards, size), F32),
             jax.ShapeDtypeStruct((queries, candidates.shape[1] * seqs), F32),
         ),
-        in_specs=[pl.BlockSpec(memory_space=pltpu.SMEM)] + [pl.BlockSpec(memory_space=pl.ANY)] * 5,
-        out_specs=(pl.BlockSpec(memory_space=pl.ANY), pl.BlockSpec(memory_space=pltpu.VMEM)),
+        in_specs=[pl.BlockSpec(memory_space=pltpu.HBM)] * 6,
+        out_specs=(pl.BlockSpec(memory_space=pltpu.VMEM), pl.BlockSpec(memory_space=pltpu.VMEM)),
         scratch_shapes=[
+            pltpu.SMEM(candidates.shape, jnp.int32),
             vmem((seqs * tokens, depth), BF16),
             vmem((seqs * tokens, depth), BF16),
             vmem((rank, depth), BF16),
@@ -274,28 +319,42 @@
             vmem((total, size), BF16),
             vmem((rank, seqs * tokens), F32),
             vmem((2 * queries, size), BF16),
-            vmem((size // shards, size), F32),
             vmem((modules, queries, 128), F32),
             dma((CHUNKS, 4)),
             dma,
             dma,
-            dma((NZ,)),
+            dma,
             dma((GROUPS, NZ)),
+            dma((GROUPS, len(WAVES))),
+            dma((GROUPS,)),
             dma,
             dma((modules,)),
-            dma((4,)),
         ],
         compiler_params=pltpu.CompilerParams(
             collective_id=0, has_side_effects=True, vmem_limit_bytes=48 * 2**20
         ),
     )(
-        candidates,
-        activations.reshape(seqs * tokens, depth),
-        out_grads.reshape(seqs * tokens, depth),
-        proj_in.reshape(rank, depth),
-        proj_out.reshape(rank, depth),
-        query_feat.reshape(queries, size),
+        *(
+            pltpu.with_memory_space_constraint(operand, pltpu.HBM)
+            for operand in (
+                candidates,
+                activations.reshape(seqs * tokens, depth),
+                out_grads.reshape(seqs * tokens, depth),
+                proj_in.reshape(rank, depth),
+                proj_out.reshape(rank, depth),
+                query_feat.reshape(queries, size),
+            )
+        ),
     )
+    gram, influence = pl.pallas_call(
+        write_kernel,
+        name="write",
+        out_shape=(jax.ShapeDtypeStruct(gram.shape, F32), jax.ShapeDtypeStruct(influence.shape, F32)),
+        in_specs=[pl.BlockSpec(memory_space=pltpu.VMEM)] * 2,
+        out_specs=[pl.BlockSpec(memory_space=pltpu.HBM)] * 2,
+        scratch_shapes=[dma, dma],
+        compiler_params=pltpu.CompilerParams(vmem_limit_bytes=2**20),
+    )(gram, influence)
     return gram[None], influence
 
 

time: 53.1 us -> 39 us (0.73)
  local copies, waits for them, and re-layouts: 7.97 us -> 0 us
  Pallas kernels: 44.2 us -> 38.2 us
    unnamed x14 -> x0, local copies, waits for them, and re-layouts: 7.97 us -> none
    pallas_call x1, Pallas kernels: 44.2 us -> 37.2 us  [on_device(): pl.pallas_call(kernel, name='influence', out_shape=(jax.ShapeDtypeStruct(...]
    pallas_call x0 -> x1, Pallas kernels: none -> 0.99 us  [on_device(): pl.pallas_call(write_kernel, name='write', out_shape=(jax.ShapeDtypeStruc...]
where the time goes in v1:
time: 39 us; the launch traced here: 38.8 us
  Pallas kernels  38.2 us (98%)
  between operations  0.64 us (2%)
    pallas_call x1, Pallas kernels, on_device(): pl.pallas_call(kernel, name='influence', out_shape=(jax.ShapeDtypeStruct(...  37.2 us
    pallas_call x1, Pallas kernels, on_device(): pl.pallas_call(write_kernel, name='write', out_shape=(jax.ShapeDtypeStruc...  0.99 us

profile of v1, /device:TPU:1, one launch (start us, length us, event | category | flops | bytes accessed | tf_op | source)
XLA Modules:
  0.0 38.8 jit_solution(3943431143697135727)
XLA Ops:
  0.6 37.2 %influence.1 = (f32[64,4096]{1,0:T(8,128)S(1)}, f32[16,16]{1,0:T(8,128)S(1)}) custom-call(s32[1,8]{1,0:T(1,128)} %cand_hbm.1, bf16[128,5120]{1,0:T(8,128)(2,1)} %bitcast.6, bf16[128,5120]{1,0:T(8,128)(2,1)} %bitcast.7, bf16[64,5120]{1,0:T(8,128)(2,1)} %bitcast.8, bf16[64,5120]{1,0:T(8,128)(2,1)} %bitcast.9, f32[16,4096]{1,0:T(8,128)} %bitcast.10), custom_call_target="tpu_custom_call" | custom-call | tf_op jit(solution)/shard_map/influence/pallas_call | solution.py:301
  37.8 1.0 %write.1 = (f32[64,4096]{1,0:T(8,128)}, f32[16,16]{1,0:T(8,128)}) custom-call(f32[64,4096]{1,0:T(8,128)S(1)} %get-tuple-element.6.gram_ref, f32[16,16]{1,0:T(8,128)S(1)} %get-tuple-element.7.infl_ref), custom_call_target="tpu_custom_call" | custom-call | tf_op jit(solution)/shard_map/write/pallas_call | solution.py:349

commit v2 on v1

--- a/solution.py
+++ b/solution.py
@@ -14,10 +14,10 @@
 MESH = pl.DeviceIdType.MESH
 F32 = jnp.float32
 BF16 = jnp.bfloat16
-X_ORDER = (1, 3, 2)
+X_ORDER = (2, 1, 3)
 SLOTS = (0, 1, 7, 2, 6, 3, 5, 4)
-DIRECT = (1, 7)
-WAVES = ((2, 6), (3, 5, 4))
+NEAR = (1, 7)
+WAVES = ((2, 6, 3, 5, 4),)
 
 
 def dot_nt(lhs, rhs):
@@ -36,8 +36,8 @@
 def kernel(
     cand_hbm, act_hbm, grad_hbm, pin_hbm, pout_hbm, query_hbm,
     gram_ref, infl_ref,
-    cand, act, grad, pin, pout, query, raw, wide, feats, turned, lhs_query, parts,
-    in_sem, query_sem, cand_sem, send_sem, block_sem, wave_sem, relay_sem, part_send, part_sem,
+    cand, act, grad, pin, pout, query, raw, wide, feats, turned, lhs_query, pick, parts,
+    in_sem, query_sem, cand_sem, send_sem, relay_send, block_sem, wave_sem, relay_sem, part_send, part_sem,
 ):
     dp = lax.axis_index("dp")
     mp = lax.axis_index("mp")
@@ -73,9 +73,6 @@
         pl.semaphore_signal(barrier, 1, device_id=dp_at(z_peer[step], group), device_id_type=MESH)
     for step in range(1, NX):
         pl.semaphore_signal(barrier, 1, device_id=dp_at(zi, x_peer[step]), device_id_type=MESH)
-    for distance in DIRECT:
-        for step in range(1, NX):
-            pl.semaphore_signal(barrier, 1, device_id=dp_at(z_peer[distance], x_peer[step]), device_id_type=MESH)
     pl.semaphore_signal(barrier, 1, device_id=mate, device_id_type=MESH)
     for step in range(1, modules):
         pl.semaphore_signal(barrier, 1, device_id={"mp": m_peer[step]}, device_id_type=MESH)
@@ -109,41 +106,55 @@
         jnp.where(lane < rank, joined[:half, s * 2 * rank:(s + 1) * 2 * rank], joined[half:, s * 2 * rank:(s + 1) * 2 * rank])
         for s in range(2)
     ]
-    raw[group * NZ] = jnp.concatenate(own, axis=0).astype(BF16)
-
-    pl.semaphore_wait(barrier, (NZ - 1) + (1 + len(DIRECT)) * (NX - 1) + 1 + (modules - 1))
+    raw[xi * NZ] = jnp.concatenate(own, axis=0).astype(BF16)
+
+    pl.semaphore_wait(barrier, (NZ - 1) + (NX - 1) + 1 + (modules - 1))
+
+    rows = half
+    seqs = GROUPS * NZ * 2
+    group_rows = NZ * 2 * rows
+    group_seqs = NZ * 2
+
+    def seqs_of(x, other):
+        return pl.ds(pl.multiple_of(other * (seqs // 2) + x * group_seqs, group_seqs), group_seqs)
+
+    def lay_out(place, x):
+        base = place * group_rows
+        wide[base:base + group_rows] = raw[pl.ds(x * NZ, NZ)].reshape(group_rows, 2 * rank).astype(F32)
+        for r in range(rows):
+            feats[seqs_of(x, 0), r * 128:(r + 1) * 128] = wide[pl.ds(base + r, group_seqs, stride=rows), :].astype(BF16)
 
     def remote(src, dst, target, arrival):
         return pltpu.make_async_remote_copy(
             src_ref=src, dst_ref=dst, send_sem=send_sem, recv_sem=arrival, device_id=target, device_id_type=MESH
         )
 
-    def blocks(g, first, count):
-        return raw.at[pl.ds(g * NZ + first, count)]
+    def blocks(x, first, count):
+        return raw.at[pl.ds(x * NZ + first, count)]
 
     def send_own(distance, step):
         slot = SLOTS.index(distance)
         target = dp_at(z_peer[(NZ - distance) % NZ], x_peer[step])
-        remote(blocks(group, 0, 1), blocks(group, slot, 1), target, block_sem.at[group, slot]).start()
-
-    def wait_block(g, slot):
-        remote(blocks(g, slot, 1), blocks(g, slot, 1), mate, block_sem.at[g, slot]).wait_recv()
-
-    def wave(g, number, target):
+        remote(blocks(xi, 0, 1), blocks(xi, slot, 1), target, block_sem.at[xi, slot]).start()
+
+    def wait_block(x, slot):
+        remote(blocks(x, slot, 1), blocks(x, slot, 1), mate, block_sem.at[x, slot]).wait_recv()
+
+    def wave(x, number, target):
         slots = [SLOTS.index(distance) for distance in WAVES[number]]
-        at = blocks(g, slots[0], len(slots))
-        return remote(at, at, target, wave_sem.at[g, number])
-
-    def relay(g):
-        return remote(blocks(g, 0, NZ), blocks(g, 0, NZ), mate, relay_sem.at[g])
+        at = blocks(x, slots[0], len(slots))
+        return remote(at, at, target, wave_sem.at[x, number])
+
+    def relay(x):
+        return pltpu.make_async_remote_copy(
+            src_ref=feats.at[seqs_of(x, 0)], dst_ref=feats.at[seqs_of(x, 1)], send_sem=relay_send,
+            recv_sem=relay_sem.at[x], device_id=mate, device_id_type=MESH,
+        )
 
     for step in X_ORDER:
         send_own(0, step)
     for distance in (4, 3, 5, 2, 6, 1, 7):
         send_own(distance, 0)
-    for distance in DIRECT:
-        for step in X_ORDER:
-            send_own(distance, step)
     query_load.wait()
     cand_load.wait()
     query_high, query_low = high_low(query[...])
@@ -151,45 +162,67 @@
     lhs_query[16:, :] = query_low
     query_sq = jnp.sum(query[...] * query[...], axis=1, keepdims=True)
 
-    rows = half
-    seqs = GROUPS * NZ * 2
-    group_rows = NZ * 2 * rows
-    group_seqs = NZ * 2
-
-    def lay_out(place, g):
-        base = place * group_rows
-        wide[base:base + group_rows] = raw[pl.ds(g * NZ, NZ)].reshape(group_rows, 2 * rank).astype(F32)
-        at = pl.ds(pl.multiple_of(g * group_seqs, group_seqs), group_seqs)
-        for r in range(rows):
-            feats[at, r * 128:(r + 1) * 128] = wide[pl.ds(base + r, group_seqs, stride=rows), :].astype(BF16)
-
+    col = lax.broadcasted_iota(jnp.int32, (seqs, 128), 1)
+    spot = jnp.full((seqs, 128), -1, jnp.int32)
+    cands = cand.shape[1]
+    for i in range(cands):
+        shard = cand[0, i]
+        distance = (shard // GROUPS + NZ - zi) % NZ
+        slot = 0
+        for number in range(1, NZ):
+            slot = jnp.where(distance == SLOTS[number], number, slot)
+        place = shard % GROUPS
+        first = (place % NC + NC - core) % NC * (seqs // 2) + place // NC * group_seqs + slot * 2
+        spot = jnp.where(col // 2 == i, first + col % 2, spot)
+    pick[...] = jnp.where(lax.broadcasted_iota(jnp.int32, (seqs, 128), 0) == spot, 1.0, 0.0).astype(BF16)
+
+    for step in X_ORDER:
+        x = (xi + step) % NX
+        wait_block(x, 0)
+        for distance in NEAR:
+            slot = SLOTS.index(distance)
+            target = dp_at(z_peer[(NZ - distance) % NZ], group)
+            remote(blocks(x, 0, 1), blocks(x, slot, 1), target, block_sem.at[x, slot]).start()
     for number in range(len(WAVES)):
         for distance in WAVES[number]:
-            wait_block(group, SLOTS.index(distance))
+            wait_block(xi, SLOTS.index(distance))
         for step in X_ORDER:
-            wave(group, number, dp_at(zi, x_peer[step])).start()
-    for distance in DIRECT:
-        wait_block(group, SLOTS.index(distance))
-    relay(group).start()
-    lay_out(0, group)
+            wave(xi, number, dp_at(zi, x_peer[step])).start()
+    for distance in NEAR:
+        wait_block(xi, SLOTS.index(distance))
+    lay_out(0, xi)
+    relay(xi).start()
     for place, step in enumerate(X_ORDER):
-        g = x_peer[step]
-        wait_block(g, 0)
-        for distance in DIRECT:
-            wait_block(g, SLOTS.index(distance))
+        x = (xi + step) % NX
+        for distance in NEAR:
+            wait_block(x, SLOTS.index(distance))
         for number in range(len(WAVES)):
-            wave(g, number, mate).wait_recv()
-        relay(g).start()
-        lay_out(1 + place, g)
-    for place, step in enumerate((0,) + X_ORDER):
-        g = ((xi + step) % NX) * NC + (1 - core)
-        relay(g).wait_recv()
-        lay_out(NX + place, g)
-
-    tile = feats[...]
-    inner = dot_nt(jnp.concatenate([tile, lhs_query[...]], axis=0), tile)
-    kmat = inner[:seqs]
-    u = inner[seqs:seqs + 16] + inner[seqs + 16:]
+            wave(x, number, mate).wait_recv()
+        lay_out(1 + place, x)
+        relay(x).start()
+
+    own_seqs = seqs // 2
+    tile = feats[:own_seqs]
+    inner_own = dot_nt(jnp.concatenate([tile, lhs_query[...]], axis=0), tile)
+    for step in (0,) + X_ORDER:
+        relay((xi + step) % NX).wait_recv()
+    other = feats[own_seqs:]
+    inner_other = dot_nt(jnp.concatenate([feats[...], lhs_query[...]], axis=0), other)
+    cross = inner_other[:own_seqs]
+    kmat = jnp.concatenate(
+        [
+            jnp.concatenate([inner_own[:own_seqs], cross], axis=1),
+            jnp.concatenate([cross.T, inner_other[own_seqs:seqs]], axis=1),
+        ],
+        axis=0,
+    )
+    u = jnp.concatenate(
+        [
+            inner_own[own_seqs:own_seqs + 16] + inner_own[own_seqs + 16:],
+            inner_other[seqs:seqs + 16] + inner_other[seqs + 16:],
+        ],
+        axis=1,
+    )
     eye = lax.broadcasted_iota(jnp.int32, (seqs, seqs), 0) == lax.broadcasted_iota(jnp.int32, (seqs, seqs), 1)
     trace = jnp.sum(jnp.sum(jnp.where(eye, kmat, 0.0), axis=1, keepdims=True), axis=0, keepdims=True)
     damping = 0.1 * trace / (rows * 2 * rank)
@@ -227,19 +260,9 @@
         dir_sq = next_sq + beta * beta * dir_sq
         resid_sq = next_sq
 
-    col = lax.broadcasted_iota(jnp.int32, (seqs, 128), 1)
-    spot = jnp.full((seqs, 128), -1, jnp.int32)
-    cands = cand.shape[1]
-    for i in range(cands):
-        shard = cand[0, i]
-        distance = (shard // GROUPS + NZ - zi) % NZ
-        slot = jnp.where(distance == 0, 0, jnp.where(distance <= NZ // 2, 2 * distance - 1, 2 * (NZ - distance)))
-        first = (shard % GROUPS) * group_seqs + slot * 2
-        spot = jnp.where(col // 2 == i, first + col % 2, spot)
-    pick = jnp.where(lax.broadcasted_iota(jnp.int32, (seqs, 128), 0) == spot, 1.0, 0.0).astype(BF16)
     s_high, s_low = high_low(scores)
     s_last = (scores - s_high.astype(F32) - s_low.astype(F32)).astype(BF16)
-    picked = dot_nn(jnp.concatenate([s_high, s_low, s_last], axis=0), pick)
+    picked = dot_nn(jnp.concatenate([s_high, s_low, s_last], axis=0), pick[...])
     picked = picked[:16] + picked[16:32] + picked[32:]
     part_col = lax.broadcasted_iota(jnp.int32, (16, 128), 1)
     parts[mp] = jnp.where(part_col == 2 * cands, selfterm, picked)
@@ -274,9 +297,10 @@
             device_id=mate, device_id_type=MESH,
         ).wait_send()
 
-    own_copies = (NX - 1) + (NZ - 1) + len(DIRECT) * (NX - 1)
+    own_copies = (NX - 1) + (NZ - 1) + len(NEAR) * (NX - 1)
     wave_copies = sum(len(distances) for distances in WAVES) * (NX - 1)
-    all_sent(raw, own_copies + wave_copies + NX * NZ, send_sem)
+    all_sent(raw, own_copies + wave_copies, send_sem)
+    all_sent(feats, seqs // 2, relay_send)
     all_sent(parts, modules - 1, part_send)
 
 
@@ -314,19 +338,21 @@
             vmem((rank, depth), BF16),
             vmem((rank, depth), BF16),
             vmem((queries, size), F32),
-            vmem((GROUPS * NZ, seqs * size // 128, 128), BF16),
-            vmem((total * size // 128, 128), F32),
+            vmem((NX * NZ, seqs * size // 128, 128), BF16),
+            vmem((total // NC * size // 128, 128), F32),
             vmem((total, size), BF16),
             vmem((rank, seqs * tokens), F32),
             vmem((2 * queries, size), BF16),
+            vmem((total, 128), BF16),
             vmem((modules, queries, 128), F32),
             dma((CHUNKS, 4)),
             dma,
             dma,
             dma,
-            dma((GROUPS, NZ)),
-            dma((GROUPS, len(WAVES))),
-            dma((GROUPS,)),
+            dma,
+            dma((NX, NZ)),
+            dma((NX, len(WAVES))),
+            dma((NX,)),
             dma,
             dma((modules,)),
         ],

time: 39 us -> 38.2 us (0.979)
  Pallas kernels: 38.2 us -> 37.5 us
    pallas_call x1, Pallas kernels: 37.2 us -> 36.5 us  [on_device(): pl.pallas_call(kernel, name='influence', out_shape=(jax.ShapeDtypeStruct(...]
where the time goes in v2:
time: 38.2 us; the launch traced here: 38.1 us
  Pallas kernels  37.5 us (98%)
  between operations  0.64 us (2%)
    pallas_call x1, Pallas kernels, on_device(): pl.pallas_call(kernel, name='influence', out_shape=(jax.ShapeDtypeStruct(...  36.5 us
    pallas_call x1, Pallas kernels, on_device(): pl.pallas_call(write_kernel, name='write', out_shape=(jax.ShapeDtypeStruc...  0.99 us

profile of v2, /device:TPU:1, one launch (start us, length us, event | category | flops | bytes accessed | tf_op | source)
XLA Modules:
  0.0 38.1 jit_solution(14721611540019011619)
XLA Ops:
  0.6 36.5 %influence.1 = (f32[64,4096]{1,0:T(8,128)S(1)}, f32[16,16]{1,0:T(8,128)S(1)}) custom-call(s32[1,8]{1,0:T(1,128)} %cand_hbm.1, bf16[128,5120]{1,0:T(8,128)(2,1)} %bitcast.6, bf16[128,5120]{1,0:T(8,128)(2,1)} %bitcast.7, bf16[64,5120]{1,0:T(8,128)(2,1)} %bitcast.8, bf16[64,5120]{1,0:T(8,128)(2,1)} %bitcast.9, f32[16,4096]{1,0:T(8,128)} %bitcast.10), custom_call_target="tpu_custom_call" | custom-call | tf_op jit(solution)/shard_map/influence/pallas_call | solution.py:325
  37.1 1.0 %write.1 = (f32[64,4096]{1,0:T(8,128)}, f32[16,16]{1,0:T(8,128)}) custom-call(f32[64,4096]{1,0:T(8,128)S(1)} %get-tuple-element.6.gram_ref, f32[16,16]{1,0:T(8,128)S(1)} %get-tuple-element.7.infl_ref), custom_call_target="tpu_custom_call" | custom-call | tf_op jit(solution)/shard_map/write/pallas_call | solution.py:375

commit v3 on v2

--- a/solution.py
+++ b/solution.py
@@ -160,7 +160,8 @@
     query_high, query_low = high_low(query[...])
     lhs_query[:16, :] = query_high
     lhs_query[16:, :] = query_low
-    query_sq = jnp.sum(query[...] * query[...], axis=1, keepdims=True)
+    query_norm = jnp.sum(query[...] * query[...], axis=1, keepdims=True)
+    query_sq = jnp.broadcast_to(query_norm, (16, 128)).T[:1]
 
     col = lax.broadcasted_iota(jnp.int32, (seqs, 128), 1)
     spot = jnp.full((seqs, 128), -1, jnp.int32)
@@ -227,13 +228,17 @@
     trace = jnp.sum(jnp.sum(jnp.where(eye, kmat, 0.0), axis=1, keepdims=True), axis=0, keepdims=True)
     damping = 0.1 * trace / (rows * 2 * rank)
     k_high, k_low = high_low(kmat)
-    k_both = jnp.concatenate([k_high, k_low], axis=1)
+    k_both = jnp.concatenate([k_high, k_low], axis=0)
 
     def apply_k(v):
         v_high, v_low = high_low(v)
-        out = dot_nn(jnp.concatenate([v_high, v_low], axis=0), k_both)
-        return out[:16, :seqs] + (out[:16, seqs:] + out[16:, :seqs])
-
+        out = dot_nn(k_both, v_high)
+        return out[:seqs] + (out[seqs:] + dot_nn(k_high, v_low))
+
+    def over_seqs(terms):
+        return jnp.sum(terms, axis=0, keepdims=True)
+
+    u = u.T
     w, v = u, u
     y = jnp.zeros_like(u)
     y_dir = jnp.zeros_like(u)
@@ -243,7 +248,7 @@
     scores = jnp.zeros_like(u)
     selfterm = jnp.zeros_like(query_sq)
     for iteration in range(ITERS):
-        alpha = resid_sq / (jnp.sum(v * v, axis=1, keepdims=True) + damping * dir_sq)
+        alpha = resid_sq / (over_seqs(v * v) + damping * dir_sq)
         scores = scores + alpha * v
         selfterm = selfterm + alpha * resid_sq
         if iteration == ITERS - 1:
@@ -252,7 +257,7 @@
         w = w - alpha * image
         y = y - alpha * (v + damping * y_dir)
         c = c - alpha * damping * c_dir
-        next_sq = c * c * query_sq + jnp.sum(y * (c * u + w), axis=1, keepdims=True)
+        next_sq = c * c * query_sq + over_seqs(y * (c * u + w))
         beta = next_sq / resid_sq
         v = w + beta * v
         y_dir = y + beta * y_dir
@@ -260,6 +265,8 @@
         dir_sq = next_sq + beta * beta * dir_sq
         resid_sq = next_sq
 
+    scores = scores.T
+    selfterm = jnp.broadcast_to(selfterm, (128, 16)).T
     s_high, s_low = high_low(scores)
     s_last = (scores - s_high.astype(F32) - s_low.astype(F32)).astype(BF16)
     picked = dot_nn(jnp.concatenate([s_high, s_low, s_last], axis=0), pick[...])

time: 38.2 us -> 38.3 us (level)
  no operation moved by 1% of the time
where the time goes in v3:
time: 38.3 us; the launch traced here: 38.2 us
  Pallas kernels  37.6 us (98%)
  between operations  0.64 us (2%)
    pallas_call x1, Pallas kernels, on_device(): pl.pallas_call(kernel, name='influence', out_shape=(jax.ShapeDtypeStruct(...  36.6 us
    pallas_call x1, Pallas kernels, on_device(): pl.pallas_call(write_kernel, name='write', out_shape=(jax.ShapeDtypeStruc...  0.99 us

profile of v3, /device:TPU:1, one launch (start us, length us, event | category | flops | bytes accessed | tf_op | source)
XLA Modules:
  0.0 38.2 jit_solution(2907508170371406655)
XLA Ops:
  0.6 36.6 %influence.1 = (f32[64,4096]{1,0:T(8,128)S(1)}, f32[16,16]{1,0:T(8,128)S(1)}) custom-call(s32[1,8]{1,0:T(1,128)} %cand_hbm.1, bf16[128,5120]{1,0:T(8,128)(2,1)} %bitcast.6, bf16[128,5120]{1,0:T(8,128)(2,1)} %bitcast.7, bf16[64,5120]{1,0:T(8,128)(2,1)} %bitcast.8, bf16[64,5120]{1,0:T(8,128)(2,1)} %bitcast.9, f32[16,4096]{1,0:T(8,128)} %bitcast.10), custom_call_target="tpu_custom_call" | custom-call | tf_op jit(solution)/shard_map/influence/pallas_call | solution.py:332
  37.2 1.0 %write.1 = (f32[64,4096]{1,0:T(8,128)}, f32[16,16]{1,0:T(8,128)}) custom-call(f32[64,4096]{1,0:T(8,128)S(1)} %get-tuple-element.6.gram_ref, f32[16,16]{1,0:T(8,128)S(1)} %get-tuple-element.7.infl_ref), custom_call_target="tpu_custom_call" | custom-call | tf_op jit(solution)/shard_map/write/pallas_call | solution.py:382

commit v4 on v3

--- a/solution.py
+++ b/solution.py
@@ -56,9 +56,7 @@
         for copy in row:
             copy.start()
     query_load = pltpu.make_async_copy(query_hbm, query, query_sem)
-    query_load.start()
     cand_load = pltpu.make_async_copy(cand_hbm, cand, cand_sem)
-    cand_load.start()
 
     def dp_at(z, g):
         return {"dp": z * GROUPS + g}
@@ -88,6 +86,9 @@
         loads[chunk][3].wait()
         pin_cols = pin[:, cols]
         xin += dot_nt(act[:, cols], jnp.concatenate([pin_cols, pin_cols], axis=0))
+
+    query_load.start()
+    cand_load.start()
 
     rank = pout.shape[0]
     half = rank // 2
@@ -153,7 +154,7 @@
 
     for step in X_ORDER:
         send_own(0, step)
-    for distance in (4, 3, 5, 2, 6, 1, 7):
+    for distance in (1, 7, 2, 6, 3, 5, 4):
         send_own(distance, 0)
     query_load.wait()
     cand_load.wait()
@@ -273,7 +274,7 @@
     picked = picked[:16] + picked[16:32] + picked[32:]
     part_col = lax.broadcasted_iota(jnp.int32, (16, 128), 1)
     parts[mp] = jnp.where(part_col == 2 * cands, selfterm, picked)
-    for step in range(1, modules):
+    for step in sorted(range(1, modules), key=lambda step: -min(step, modules - step)):
         pltpu.make_async_remote_copy(
             src_ref=parts.at[mp], dst_ref=parts.at[mp], send_sem=part_send, recv_sem=part_sem.at[mp],
             device_id={"mp": m_peer[step]}, device_id_type=MESH,

time: 38.3 us -> 37.3 us (0.974)
  Pallas kernels: 37.6 us -> 36.5 us
    pallas_call x1, Pallas kernels: 36.6 us -> 35.5 us  [on_device(): pl.pallas_call(kernel, name='influence', out_shape=(jax.ShapeDtypeStruct(...]
where the time goes in v4:
time: 37.3 us; the launch traced here: 37.2 us
  Pallas kernels  36.5 us (98%)
  between operations  0.64 us (2%)
    pallas_call x1, Pallas kernels, on_device(): pl.pallas_call(kernel, name='influence', out_shape=(jax.ShapeDtypeStruct(...  35.5 us
    pallas_call x1, Pallas kernels, on_device(): pl.pallas_call(write_kernel, name='write', out_shape=(jax.ShapeDtypeStruc...  0.99 us

profile of v4, /device:TPU:1, one launch (start us, length us, event | category | flops | bytes accessed | tf_op | source)
XLA Modules:
  0.0 37.2 jit_solution(8695600859567001860)
XLA Ops:
  0.6 35.5 %influence.1 = (f32[64,4096]{1,0:T(8,128)S(1)}, f32[16,16]{1,0:T(8,128)S(1)}) custom-call(s32[1,8]{1,0:T(1,128)} %cand_hbm.1, bf16[128,5120]{1,0:T(8,128)(2,1)} %bitcast.6, bf16[128,5120]{1,0:T(8,128)(2,1)} %bitcast.7, bf16[64,5120]{1,0:T(8,128)(2,1)} %bitcast.8, bf16[64,5120]{1,0:T(8,128)(2,1)} %bitcast.9, f32[16,4096]{1,0:T(8,128)} %bitcast.10), custom_call_target="tpu_custom_call" | custom-call | tf_op jit(solution)/shard_map/influence/pallas_call | solution.py:333
  36.2 1.0 %write.1 = (f32[64,4096]{1,0:T(8,128)}, f32[16,16]{1,0:T(8,128)}) custom-call(f32[64,4096]{1,0:T(8,128)S(1)} %get-tuple-element.6.gram_ref, f32[16,16]{1,0:T(8,128)S(1)} %get-tuple-element.7.infl_ref), custom_call_target="tpu_custom_call" | custom-call | tf_op jit(solution)/shard_map/write/pallas_call | solution.py:383
